TPU v7x, 256 devices: a whole 4x4x8 slice. The times are simulated.
256 devices in a mesh: pipe: 8 (over y, core), tensor: 8 (over x, z_hi), dp: 4 (over z_lo).
Axes of the slice: x: 4, y: 4, z: 8 (z_hi: 2, z_lo: 4; z = z_hi * 4 + z_lo), core: 2. Of those that a mesh axis runs over, the one named last changes fastest.
Arguments:
- encoder_out: bfloat16 [4, 512, 4096], P('dp', 'pipe', 'tensor'), may hold values from -6 to 6
- queries: bfloat16 [8, 4, 512, 4096], P('pipe', 'dp', None, 'tensor'), may hold values from -48 to 48
- ctx_grad: bfloat16 [8, 4, 512, 4096], P('pipe', 'dp', None, 'tensor'), may hold values from -6 to 6
- key_weight: bfloat16 [8, 4096, 4096], P('pipe', 'dp', 'tensor'), may hold values from -0.09375 to 0.09375
- value_weight: bfloat16 [8, 4096, 4096], P('pipe', 'dp', 'tensor'), may hold values from -0.09375 to 0.09375
Outputs:
- query_grad: bfloat16 [8, 4, 512, 4096], P('pipe', 'dp', None, 'tensor')
- key_weight_grad: float32 [8, 4096, 4096], P('pipe', 'dp', 'tensor')
- value_weight_grad: float32 [8, 4096, 4096], P('pipe', 'dp', 'tensor')
- encoder_grad: float32 [4, 512, 4096], P('dp', 'pipe', 'tensor')
All inputs are finite; a program needn't handle non-finite values.
Results may differ from a plain program's by a relative error of at most 0.014.
The roundings to bfloat16 on the way count: a program that leaves them out, or rounds other values in their place, can miss the bound.
Values may be sent and summed in bfloat16 or wider, within the bound.
A program may use at most 128 MiB of HBM per device.

v0:
```python
import math

import jax
import jax.numpy as jnp
from jax import lax
from jax.sharding import PartitionSpec as P

DH = 256


def shards(encoder_out, queries, ctx_grad, key_weight, value_weight):
    widened = lax.all_gather(encoder_out, "tensor", axis=2, tiled=True)
    enc_all = lax.all_gather(widened, "pipe", axis=1, tiled=True)
    wkey_all, wval_all = (
        lax.all_gather(key_weight[0], "dp", axis=0, tiled=True),
        lax.all_gather(value_weight[0], "dp", axis=0, tiled=True),
    )
    seq_count, enc_len, model_width = enc_all.shape
    dec_len = queries.shape[2]
    local_cols = wkey_all.shape[1]
    head_count = local_cols // DH
    scale_q = 1.0 / math.sqrt(DH)
    enc_flat = enc_all.reshape(seq_count * enc_len, model_width)
    key_rows = jnp.dot(enc_flat, wkey_all, preferred_element_type=jnp.float32).astype(jnp.bfloat16)
    value_rows = jnp.dot(enc_flat, wval_all, preferred_element_type=jnp.float32).astype(
        jnp.bfloat16
    )
    key_heads = key_rows.reshape(seq_count, enc_len, head_count, DH)
    value_heads = value_rows.reshape(seq_count, enc_len, head_count, DH)
    query_heads = queries[0].reshape(seq_count, dec_len, head_count, DH)
    grad_heads = ctx_grad[0].reshape(seq_count, dec_len, head_count, DH)
    scores = (
        jnp.einsum("bqhd,bkhd->bhqk", query_heads, key_heads, preferred_element_type=jnp.float32)
        * scale_q
    )
    attention = jax.nn.softmax(scores, axis=-1)
    attention_low = attention.astype(jnp.bfloat16)
    prob_grad = jnp.einsum(
        "bqhd,bkhd->bhqk", grad_heads, value_heads, preferred_element_type=jnp.float32
    )
    score_grad = attention * (prob_grad - jnp.sum(prob_grad * attention, axis=-1, keepdims=True))
    score_low = (score_grad * scale_q).astype(jnp.bfloat16)
    query_grad = jnp.einsum(
        "bhqk,bkhd->bqhd", score_low, key_heads, preferred_element_type=jnp.float32
    ).astype(jnp.bfloat16)
    query_grad = query_grad.reshape(1, seq_count, dec_len, local_cols)
    key_grad = jnp.einsum(
        "bhqk,bqhd->bkhd", score_low, query_heads, preferred_element_type=jnp.float32
    ).astype(jnp.bfloat16)
    value_grad = jnp.einsum(
        "bhqk,bqhd->bkhd", attention_low, grad_heads, preferred_element_type=jnp.float32
    ).astype(jnp.bfloat16)
    key_flat = key_grad.reshape(seq_count * enc_len, local_cols)
    value_flat = value_grad.reshape(seq_count * enc_len, local_cols)
    contract = (((0,), (0,)), ((), ()))
    key_part = lax.dot_general(enc_flat, key_flat, contract, preferred_element_type=jnp.float32)
    val_part = lax.dot_general(enc_flat, value_flat, contract, preferred_element_type=jnp.float32)
    summed = lax.psum_scatter(
        jnp.concatenate([key_part, val_part], axis=1).astype(jnp.bfloat16),
        "dp",
        scatter_dimension=0,
        tiled=True,
    ).astype(jnp.float32)
    wkey_grad = summed[:, :local_cols][None]
    wval_grad = summed[:, local_cols:][None]
    sections = lax.axis_size("pipe")
    splits = lax.axis_size("tensor")
    local_pos = enc_len // sections
    local_width = model_width // splits
    block_rows = seq_count * local_pos
    key_split = key_grad.reshape(seq_count, sections, local_pos, local_cols)
    value_split = value_grad.reshape(seq_count, sections, local_pos, local_cols)
    wkey_split = wkey_all.reshape(splits, local_width, local_cols)
    wval_split = wval_all.reshape(splits, local_width, local_cols)
    enc_term = jnp.einsum(
        "bpsh,tfh->ptbsf", key_split, wkey_split, preferred_element_type=jnp.float32
    )
    enc_term = enc_term + jnp.einsum(
        "bpsh,tfh->ptbsf", value_split, wval_split, preferred_element_type=jnp.float32
    )
    flat_term = enc_term.reshape(sections * splits * block_rows, local_width)
    enc_grad = lax.psum_scatter(flat_term, ("pipe", "tensor"), scatter_dimension=0, tiled=True)
    enc_grad = enc_grad.reshape(seq_count, local_pos, local_width)
    return (query_grad, wkey_grad, wval_grad, enc_grad)


def solution(mesh):
    in_specs = (
        P("dp", "pipe", "tensor"),
        P("pipe", "dp", None, "tensor"),
        P("pipe", "dp", None, "tensor"),
        P("pipe", "dp", "tensor"),
        P("pipe", "dp", "tensor"),
    )
    out_specs = (
        P("pipe", "dp", None, "tensor"),
        P("pipe", "dp", "tensor"),
        P("pipe", "dp", "tensor"),
        P("dp", "pipe", "tensor"),
    )
    return jax.shard_map(shards, mesh=mesh, in_specs=in_specs, out_specs=out_specs, check_vma=False)
```

profile of v0, /device:TPU:6, one launch (start us, length us, event | category | flops | bytes accessed | tf_op | source)
XLA Modules:
  0.0 892.5 jit_solution(6884369129092783502)
XLA Ops:
  7.2 0.0 copy-start.1
  7.2 0.0 copy-start.2
  7.2 0.0 all-gather.10.cloned.1.call-start
  7.2 0.7 all-gather.10.cloned.1.call-update
  7.9 0.0 all-gather.6.cloned.1.call-start
  8.0 54.0 %all_gather.12 = bf16[1,64,4096]{2,1,0:T(8,128)(2,1)} all-gather(bf16[1,64,512]{2,1,0:T(8,128)(2,1)} %param.5), channel_id=1, replica_groups=mesh['pipe'=8,'tensor'=8,'dp'=4] {'tensor'}, dimensions={2}, use_global_device_ids=true | all-gather | bytes 589824 | tf_op jit(solution)/shard_map/all_gather | solution.py:12
  62.0 0.0 all-gather.6.cloned.1.call-update
  62.0 0.0 all-gather.8.cloned.1.call-start
  62.0 0.7 all-gather.8.cloned.1.call-update
  62.7 0.0 reduce-scatter.3.cloned.1.call-start
  62.8 0.0 copy-done.1
  62.8 0.2 copy.46
  63.0 0.0 copy-done.2
  63.0 0.2 copy.47
  63.2 46.7 %all-gather.10.cloned.1.call-done = bf16[1,4096,512]{2,1,0:T(8,128)(2,1)} async-done(((bf16[1,1024,512]{2,1,0:T(8,128)(2,1)}), bf16[1,4096,512]{2,1,0:T(8,128)(2,1)}) %all-gather.10.cloned.1.call-update) | async-done | bytes 4194320 | tf_op jit(solution)/shard_map/all_gather | solution.py:16
  110.0 35.2 %all-gather.6.cloned.1.call-done = bf16[1,512,4096]{2,1,0:T(8,128)(2,1)} async-done(((bf16[1,64,4096]{2,1,0:T(8,128)(2,1)}), bf16[1,512,4096]{2,1,0:T(8,128)(2,1)}) %all-gather.6.cloned.1.call-update) | async-done | bytes 4194320 | tf_op jit(solution)/shard_map/all_gather | solution.py:13
  145.2 5.8 fusion.25
  151.0 0.5 fusion.44
  151.5 79.4 %all-gather.8.cloned.1.call-done = bf16[1,4096,512]{2,1,0:T(8,128)(2,1)} async-done(((bf16[1,1024,512]{2,1,0:T(8,128)(2,1)}), bf16[1,4096,512]{2,1,0:T(8,128)(2,1)}) %all-gather.8.cloned.1.call-update) | async-done | bytes 4194320 | tf_op jit(solution)/shard_map/all_gather | solution.py:15
  230.9 6.6 fusion.20
  237.6 3.3 fusion.43
  240.8 2.9 convolution_convert_fusion.2
  243.7 3.2 convolution_convert_fusion.3
  246.9 0.0 copy-start.3
  246.9 0.0 copy-start.5
  246.9 6.9 fusion.3
  253.8 0.0 copy-done.5
  253.8 4.3 fusion.2
  258.1 8.0 pad_maximum_fusion
  266.1 0.0 reduce-scatter.3.cloned.1.call-update
  266.1 0.0 reduce-scatter.5.cloned.1.call-start
  266.2 1.0 copy-done.4
  267.1 0.4 copy.35
  267.6 0.3 reshape.128
  267.9 1.4 copy.34
  269.3 1.1 reshape.126
  270.4 4.9 fusion.34
  275.3 5.6 convolution_add_fusion
  280.9 0.0 reduce-scatter.5.cloned.1.call-update
  280.9 1.0 copy-done.6
  281.9 3.3 convolution_convert_fusion.4
  285.2 1.0 copy.36
  286.2 130.0 %reduce-scatter.3.cloned.1.call-done = bf16[1024,1024]{0,1:T(8,128)(2,1)} async-done(((bf16[4096,1024]{0,1:T(8,128)(2,1)}), bf16[1024,1024]{0,1:T(8,128)(2,1)}) %reduce-scatter.3.cloned.1.call-update) | async-done | bytes 2097168 | tf_op jit(solution)/shard_map/reduce_scatter | solution.py:58
  416.2 2.0 convert_element_type.66
  418.3 1.8 slice_bitcast_fusion
  420.0 2.9 copy.38
  422.9 1.8 copy.37
  424.7 461.3 %reduce-scatter.5.cloned.1.call-done = f32[64,512]{1,0:T(8,128)} async-done(((f32[4096,512]{1,0:T(8,128)}), f32[64,512]{1,0:T(8,128)}) %reduce-scatter.5.cloned.1.call-update) | async-done | bytes 131088 | tf_op jit(solution)/shard_map/reduce_scatter | solution.py:82
  (5 shorter events, 0.0 us)
Async XLA Ops:
  7.2 55.6 %copy-start.1 = (bf16[1,1,512,512]{3,2,1,0:T(8,128)(2,1)S(1)}, bf16[1,1,512,512]{3,2,1,0:T(8,128)(2,1)}, u32[]{:S(2)}) copy-start(bf16[1,1,512,512]{3,2,1,0:T(8,128)(2,1)} %param.6) | copy-start | bytes 1572868
  7.2 55.8 %copy-start.2 = (bf16[1,1,512,512]{3,2,1,0:T(8,128)(2,1)S(1)}, bf16[1,1,512,512]{3,2,1,0:T(8,128)(2,1)}, u32[]{:S(2)}) copy-start(bf16[1,1,512,512]{3,2,1,0:T(8,128)(2,1)} %param.7) | copy-start | bytes 1572868
  7.2 102.8 %all-gather.10.cloned.1.call-start = ((), (), s32[]{:S(2)}) async-start(), calls=%async_computation.6 | async-start | bytes 5242880 | tf_op jit(solution)/shard_map/all_gather | solution.py:16
  7.9 137.3 %all-gather.6.cloned.1.call-start = ((), (), s32[]{:S(2)}) async-start(), calls=%async_computation.2 | async-start | bytes 4718592 | tf_op jit(solution)/shard_map/all_gather | solution.py:13
  62.0 169.0 %all-gather.8.cloned.1.call-start = ((), (), s32[]{:S(2)}) async-start(), calls=%async_computation.5 | async-start | bytes 5242880 | tf_op jit(solution)/shard_map/all_gather | solution.py:15
  62.7 353.5 %reduce-scatter.3.cloned.1.call-start = ((), (), s32[]{:S(2)}) async-start(), calls=%async_computation.3 | async-start | bytes 10485760 | tf_op jit(solution)/shard_map/reduce_scatter | solution.py:58
  246.9 6.9 copy-start.3
  246.9 6.9 copy-start.5
  266.1 1.0 copy-start.4
  266.1 619.9 %reduce-scatter.5.cloned.1.call-start = ((), (), s32[]{:S(2)}) async-start(), calls=%async_computation.4 | async-start | bytes 8519680 | tf_op jit(solution)/shard_map/reduce_scatter | solution.py:82
  270.4 4.9 copy-start
  280.9 1.0 copy-start.6
Sparse Core Ops, SparseCore 0:
  9.8 100.0 all-gather.9
  111.8 33.3 all-gather.5
  147.0 83.8 all-gather.7
  266.2 149.9 reduce-scatter.2
  419.2 466.7 reduce-scatter.4
where the time goes:
time: 906 us; the launch traced here: 893 us
  waiting for transfers between devices  754 us (83%)
  blocking collectives  54 us (6%)
  matrix products  47.2 us (5%)
  between operations  13.9 us (2%)
  local copies, waits for them, and re-layouts  13.2 us (1%)
  other arithmetic  10 us (1%)
    reduce_scatter x1, waiting for transfers between devices, shards(): lax.psum_scatter(flat_term, ('pipe', 'tensor'), scatter_dimension=0, tile...  461 us
    reduce_scatter x1, waiting for transfers between devices, shards(): lax.psum_scatter(jnp.concatenate([key_part, val_part], axis=1).astype(jnp...  130 us
    all_gather x1, waiting for transfers between devices, shards(): lax.all_gather(key_weight[0], 'dp', axis=0, tiled=True)  79.4 us
    all_gather x1, blocking collectives, shards(): widened = lax.all_gather(encoder_out, 'tensor', axis=2, tiled=True)  54 us
    all_gather x1, waiting for transfers between devices, shards(): lax.all_gather(value_weight[0], 'dp', axis=0, tiled=True)  46.7 us
    all_gather x1, waiting for transfers between devices, shards(): enc_all = lax.all_gather(widened, 'pipe', axis=1, tiled=True)  35.2 us
  transfers between devices with their start and end apart: 5, of which 5 were waited for; matrix products, arithmetic and copies ran while one was open for 4% of the time, Pallas kernels for 0%

commit v1 on v0

v1 whole, which is shorter than its diff:
```python
import math

import jax
import jax.numpy as jnp
from jax import lax
from jax.experimental import pallas as pl
from jax.experimental.pallas import tpu as pltpu
from jax.sharding import PartitionSpec as P

DH = 256
BF = jnp.bfloat16
F32 = jnp.float32
MESH = pl.DeviceIdType.MESH
NT = (((1,), (1,)), ((), ()))
TN = (((0,), (0,)), ((), ()))


def mm(a, b):
    return jnp.dot(a, b, preferred_element_type=F32)


def kernel(
    enc, q, ctx, wk, wv,
    qg, gk, gv, eg,
    encg, enct, wbuf, psk, psv, prk, prv, pown, krow, vrow, sl, al, kvg,
    gsend, grecv, dacc, dsend, drecv, r1, ra_a, ra_b, r2a, r2b, rb_a, rb_b, fin, frecv,
    ssem, rsem, lsem,
):
    pi = lax.axis_index("pipe")
    ti = lax.axis_index("tensor")
    d = lax.axis_index("dp")
    y, c = pi // 2, pi % 2
    x, zh = ti // 2, ti % 2
    xh, xl = x // 2, x % 2
    dh, dl = d // 2, d % 2
    oc, oh, ol = 1 - c, 1 - dh, 1 - dl
    scale = 1.0 / math.sqrt(DH)

    def xpeer(k):
        xx = (x + k) % 4
        return (pi, xx * 2 + zh, d)

    def ypeer(k):
        yy = (y + k) % 4
        return (yy * 2 + c, ti, d)

    peer_c = (y * 2 + oc, ti, d)
    peer_l = (pi, ti, dh * 2 + ol)
    peer_h = (pi, ti, oh * 2 + dl)
    tx = dh * 2 + xl
    td = xh * 2 + dl
    peer_t0 = (pi, tx * 2 + zh, td)
    peer_t1 = (pi, tx * 2 + 1 - zh, td)
    home = xh == dh

    used = [0]

    def send(src, dst, dev):
        k = used[0]
        used[0] += 1
        return pltpu.make_async_remote_copy(
            src, dst, ssem.at[k], rsem.at[k], device_id=dev, device_id_type=MESH
        )

    peers = [peer_c, peer_l, peer_h, peer_t1]
    peers += [xpeer(k) for k in (1, 2, 3)] + [ypeer(k) for k in (1, 2, 3)]
    barrier = pltpu.get_barrier_semaphore()
    for dev in peers:
        pl.semaphore_signal(barrier, inc=1, device_id=dev, device_id_type=MESH)

    @pl.when(jnp.logical_not(home))
    def _():
        pl.semaphore_signal(barrier, inc=1, device_id=peer_t0, device_id_type=MESH)

    owns = []
    for h in range(2):
        for kv, w in enumerate((wk, wv)):
            cp = pltpu.make_async_copy(
                w.at[:, pl.ds(h * DH, DH)], wbuf.at[h, kv, dl], lsem.at[h * 2 + kv]
            )
            cp.start()
            owns.append(cp)

    @pl.when(home)
    def _():
        pl.semaphore_wait(barrier, len(peers))

    @pl.when(jnp.logical_not(home))
    def _():
        pl.semaphore_wait(barrier, len(peers) + 1)

    piece = encg.at[dh, xl * 2 + zh, y, c]
    to_t0 = send(enc, piece, peer_t0)
    to_t1 = send(enc, piece, peer_t1)
    to_t1.start()

    @pl.when(home)
    def _():
        encg[dh, xl * 2 + zh, y, c] = enc[...]

    @pl.when(jnp.logical_not(home))
    def _():
        to_t0.start()

    wsend = [
        [send(w.at[:, pl.ds(h * DH, DH)], wbuf.at[h, kv, dl], peer_l) for kv, w in enumerate((wk, wv))]
        for h in range(2)
    ]
    for cp in wsend[0]:
        cp.start()

    to_t1.wait()

    @pl.when(jnp.logical_not(home))
    def _():
        to_t0.wait()

    xa = pl.ds(xl * 2, 2)
    lo, hi = pl.ds(0, 32), pl.ds(32, 32)
    first = []
    for k in (1, 2, 3):
        ref = encg.at[xh, xa, y, c, lo]
        first.append(send(ref, ref, xpeer(k)))
        ref = encg.at[xh, xa, y, c, hi]
        first.append(send(ref, ref, ypeer(k)))
    for cp in first:
        cp.start()
    for cp in first:
        cp.wait()
    second = []
    for k in (1, 2, 3):
        ref = encg.at[:, :, y, c, lo]
        second.append(send(ref, ref, ypeer(k)))
        ref = encg.at[xh, xa, :, c, hi]
        second.append(send(ref, ref, xpeer(k)))
    for cp in second:
        cp.start()
    for cp in wsend[1]:
        cp.start()
    for cp in second:
        cp.wait()
    third = []
    for s in (oh, dh):
        ref = encg.at[s, :, :, c]
        third.append(send(ref, ref, peer_c))
    for cp in third:
        cp.start()

    def enc_rows(s, r):
        blocks = [encg[s, fb, pl.ds(r * 2, 2)].reshape(256, 512) for fb in range(4)]
        return jnp.concatenate(blocks, axis=1)

    def project(s, h, kv, put):
        def step(r, carry):
            w = wbuf[h, kv].reshape(2048, DH)
            put(pl.ds(pl.multiple_of(r * 256, 256), 256), mm(enc_rows(s, r), w))
            return carry

        lax.fori_loop(0, 2, step, 0)

    def put_k(h):
        def put(rows, v):
            psk[h, rows, :] = v

        return put

    def put_v(h):
        def put(rows, v):
            psv[h, rows, :] = v.astype(BF)

        return put

    def put_own(h, kv):
        def put(rows, v):
            pown[h, kv, rows, :] = v

        return put

    part = []
    for h in range(2):
        for kv in range(2):
            owns[h * 2 + kv].wait()
            wsend[h][kv].wait()
            if h == 0 and kv == 0:
                third[0].wait()
            if kv == 0:
                project(oh, h, 0, put_k(h))
                cp = send(psk.at[h], prk.at[h], peer_h)
            else:
                project(oh, h, 1, put_v(h))
                cp = send(psv.at[h], prv.at[h], peer_h)
            cp.start()
            part.append(cp)
        if h == 0:
            third[1].wait()
        for kv in range(2):
            project(dh, h, kv, put_own(h, kv))

    def flip(n, carry):
        s, fb = n // 4, n % 4
        enct[s, fb] = encg[s, fb].reshape(512, 512).T
        return carry

    lax.fori_loop(0, 8, flip, 0)

    grads = []
    for h in range(2):
        part[2 * h].wait()
        part[2 * h + 1].wait()
        krow[h] = (pown[h, 0] + prk[h]).astype(BF)
        vrow[h] = (pown[h, 1] + prv[h].astype(F32)).astype(BF)
        cols = pl.ds(h * DH, DH)

        def attend(r, carry):
            rows = pl.ds(pl.multiple_of(r * 128, 128), 128)
            kk = krow[h]
            s = lax.dot_general(q[rows, cols], kk, NT, preferred_element_type=F32) * scale
            e = jnp.exp(s - jnp.max(s, axis=-1, keepdims=True))
            a = e / jnp.sum(e, axis=-1, keepdims=True)
            p = lax.dot_general(ctx[rows, cols], vrow[h], NT, preferred_element_type=F32)
            g = a * (p - jnp.sum(p * a, axis=-1, keepdims=True))
            low = (g * scale).astype(BF)
            sl[rows, :] = low
            al[rows, :] = a.astype(BF)
            qg[rows, cols] = mm(low, kk).astype(BF)
            return carry

        lax.fori_loop(0, 4, attend, 0)
        kvg[h, dh, :, 0:DH] = lax.dot_general(
            sl[...], q[:, cols], TN, preferred_element_type=F32
        ).astype(BF)
        kvg[h, dh, :, DH : 2 * DH] = lax.dot_general(
            al[...], ctx[:, cols], TN, preferred_element_type=F32
        ).astype(BF)
        cp = send(kvg.at[h, dh], kvg.at[h, dh], peer_h)
        cp.start()
        grads.append(cp)

    def weight_rows(fb):
        qt, half = fb // 2, pl.ds(pl.multiple_of((fb % 2) * 512, 512), 512)
        return jnp.concatenate([wbuf[h, kv, qt, half, :] for h in range(2) for kv in range(2)], axis=1)

    def encoder_term(s):
        def step(fb, carry):
            both = jnp.concatenate([kvg[0, s], kvg[1, s]], axis=1)
            v = lax.dot_general(both, weight_rows(fb), NT, preferred_element_type=F32)
            dacc[s, fb] = v.reshape(4, 2, 64, 512)
            dsend[s, fb] = dacc[s, fb, :, oc].astype(BF)
            return carry

        lax.fori_loop(0, 4, step, 0)

    core = []

    def encoder_start(s):
        encoder_term(s)
        cp = send(dsend.at[s], drecv.at[s], peer_c)
        cp.start()
        core.append(cp)

    encoder_start(dh)

    def weight_term(h, qt, put):
        def step(z, carry):
            fb = qt * 2 + z
            lhs = jnp.concatenate([enct[0, fb], enct[1, fb]], axis=1)
            rhs = jnp.concatenate([kvg[h, 0], kvg[h, 1]], axis=0)
            put(pl.ds(pl.multiple_of(z * 512, 512), 512), mm(lhs, rhs))
            return carry

        lax.fori_loop(0, 2, step, 0)

    gsent = []

    def weight_send(h):
        def put(rows, v):
            gsend[h, rows, :] = v.astype(BF)

        weight_term(h, ol, put)
        cp = send(gsend.at[h], grecv.at[h], peer_l)
        cp.start()
        gsent.append(cp)

    def weight_own(h):
        cols = pl.ds(h * DH, DH)

        def put(rows, v):
            gk[rows, cols] = v[:, :DH]
            gv[rows, cols] = v[:, DH:]

        weight_term(h, dl, put)

    grads[0].wait()
    weight_send(0)
    weight_own(0)
    grads[1].wait()
    weight_send(1)
    encoder_start(oh)
    core[0].wait()

    def fold_core(s):
        def step(n, carry):
            fb, yy = n // 4, n % 4
            r1[s, fb, yy] = (dacc[s, fb, yy, c] + drecv[s, fb, yy].astype(F32)).astype(BF)
            return carry

        lax.fori_loop(0, 16, step, 0)

    fold_core(dh)
    core[1].wait()
    fold_core(oh)

    one = []
    for k in (1, 2, 3):
        xx = (x + k) % 4
        one.append(send(r1.at[xx // 2, pl.ds((xx % 2) * 2, 2), :, lo], ra_a.at[k - 1], xpeer(k)))
        one.append(send(r1.at[:, :, (y + k) % 4, hi], ra_b.at[k - 1], ypeer(k)))
    for cp in one:
        cp.start()
    weight_own(1)
    for cp in one:
        cp.wait()

    def fold_a(n, carry):
        z, yy = n // 4, n % 4
        v = r1[xh, xl * 2 + z, yy, 0:32, :].astype(F32)
        for k in range(3):
            v = v + ra_a[k, z, yy].astype(F32)
        r2a[z, yy] = v.astype(BF)
        return carry

    lax.fori_loop(0, 8, fold_a, 0)

    def fold_b(n, carry):
        s, fb = n // 4, n % 4
        v = r1[s, fb, y, 32:64, :].astype(F32)
        for k in range(3):
            v = v + ra_b[k, s, fb].astype(F32)
        r2b[s, fb] = v.astype(BF)
        return carry

    lax.fori_loop(0, 8, fold_b, 0)

    two = []
    for k in (1, 2, 3):
        xx = (x + k) % 4
        two.append(send(r2a.at[:, (y + k) % 4], rb_a.at[k - 1], ypeer(k)))
        two.append(send(r2b.at[xx // 2, pl.ds((xx % 2) * 2, 2)], rb_b.at[k - 1], xpeer(k)))
    for cp in two:
        cp.start()
    for cp in two:
        cp.wait()
    for z in range(2):
        v = r2a[z, y].astype(F32)
        for k in range(3):
            v = v + rb_a[k, z].astype(F32)
        fin[z, 0:32, :] = v
        v = r2b[xh, xl * 2 + z].astype(F32)
        for k in range(3):
            v = v + rb_b[k, z].astype(F32)
        fin[z, 32:64, :] = v
    last0 = send(fin.at[zh], frecv.at[0], peer_t0)
    last1 = send(fin.at[1 - zh], frecv.at[1], peer_t1)
    last1.start()

    @pl.when(jnp.logical_not(home))
    def _():
        last0.start()

    for h in range(2):
        gsent[h].wait()
        cols = pl.ds(h * DH, DH)

        def add(r, carry):
            rows = pl.ds(pl.multiple_of(r * 128, 128), 128)
            gk[rows, cols] += grecv[h, rows, 0:DH].astype(F32)
            gv[rows, cols] += grecv[h, rows, DH : 2 * DH].astype(F32)
            return carry

        lax.fori_loop(0, 8, add, 0)

    last1.wait()

    @pl.when(jnp.logical_not(home))
    def _():
        last0.wait()
        eg[...] = frecv[0] + frecv[1]

    @pl.when(home)
    def _():
        eg[...] = fin[zh] + frecv[1]


def shards(encoder_out, queries, ctx_grad, key_weight, value_weight):
    vm = pl.BlockSpec(memory_space=pltpu.VMEM)
    hbm = pl.BlockSpec(memory_space=pl.ANY)
    scratch = [
        ((2, 4, 4, 2, 64, 512), BF),
        ((2, 4, 512, 512), BF),
        ((2, 2, 2, 1024, DH), BF),
        ((2, 512, DH), F32),
        ((2, 512, DH), BF),
        ((2, 512, DH), F32),
        ((2, 512, DH), BF),
        ((2, 2, 512, DH), F32),
        ((2, 512, DH), BF),
        ((2, 512, DH), BF),
        ((512, 512), BF),
        ((512, 512), BF),
        ((2, 2, 512, 512), BF),
        ((2, 1024, 512), BF),
        ((2, 1024, 512), BF),
        ((2, 4, 4, 2, 64, 512), F32),
        ((2, 4, 4, 64, 512), BF),
        ((2, 4, 4, 64, 512), BF),
        ((2, 4, 4, 64, 512), BF),
        ((3, 2, 4, 32, 512), BF),
        ((3, 2, 4, 32, 512), BF),
        ((2, 4, 32, 512), BF),
        ((2, 4, 32, 512), BF),
        ((3, 2, 32, 512), BF),
        ((3, 2, 32, 512), BF),
        ((2, 64, 512), F32),
        ((2, 64, 512), F32),
    ]
    qg, gk, gv, eg = pl.pallas_call(
        kernel,
        out_shape=[
            jax.ShapeDtypeStruct((512, 512), BF),
            jax.ShapeDtypeStruct((1024, 512), F32),
            jax.ShapeDtypeStruct((1024, 512), F32),
            jax.ShapeDtypeStruct((64, 512), F32),
        ],
        in_specs=[vm, vm, vm, hbm, hbm],
        out_specs=[vm, vm, vm, vm],
        scratch_shapes=[pltpu.VMEM(*s) for s in scratch]
        + [
            pltpu.SemaphoreType.DMA((48,)),
            pltpu.SemaphoreType.DMA((48,)),
            pltpu.SemaphoreType.DMA((4,)),
        ],
        compiler_params=pltpu.CompilerParams(
            collective_id=0, has_side_effects=True, vmem_limit_bytes=60 * 1024 * 1024
        ),
        cost_estimate=pl.CostEstimate(
            flops=14_200_000_000, bytes_accessed=8_000_000, transcendentals=600_000
        ),
    )(encoder_out[0], queries[0, 0], ctx_grad[0, 0], key_weight[0], value_weight[0])
    return qg[None, None], gk[None], gv[None], eg[None]


def solution(mesh):
    in_specs = (
        P("dp", "pipe", "tensor"),
        P("pipe", "dp", None, "tensor"),
        P("pipe", "dp", None, "tensor"),
        P("pipe", "dp", "tensor"),
        P("pipe", "dp", "tensor"),
    )
    out_specs = (
        P("pipe", "dp", None, "tensor"),
        P("pipe", "dp", "tensor"),
        P("pipe", "dp", "tensor"),
        P("dp", "pipe", "tensor"),
    )
    return jax.shard_map(shards, mesh=mesh, in_specs=in_specs, out_specs=out_specs, check_vma=False)
```

time: 906 us -> 219 us (0.24); the launches traced: 893 us -> 218 us
  waiting for transfers between devices: 754 us -> 0 us
  Pallas kernels: 0 us -> 211 us
  blocking collectives: 54 us -> 0 us
  matrix products: 47.2 us -> 0 us
  between operations: 13.9 us -> 0.64 us
  other arithmetic: 10 us -> 0 us
    reduce_scatter x2 -> x0, waiting for transfers between devices: 591 us -> none  [the longest x1 461 us: shards(): lax.psum_scatter(flat_term, ('pipe', 'tensor'), scatter_dimension=0, tile...]
    pallas_call x0 -> x1, Pallas kernels: none -> 211 us  [shards(): pl.pallas_call(kernel, out_shape=[jax.ShapeDtypeStruct((512, 512), BF), j...]
    all_gather x3 -> x0, waiting for transfers between devices: 161 us -> none  [the longest x1 79.4 us: shards(): lax.all_gather(key_weight[0], 'dp', axis=0, tiled=True)]
    all_gather x1 -> x0, blocking collectives: 54 us -> none  [shards(): widened = lax.all_gather(encoder_out, 'tensor', axis=2, tiled=True)]
    dot_general x10 -> x0, matrix products: 43.9 us -> none  [the longest x1 6.86 us: shards(): lax.dot_general(enc_flat, value_flat, contract, preferred_element_type=jn...]
  transfers between devices with their start and end apart: 5 -> 0, of which waited for: 5 -> 0; matrix products, arithmetic and copies ran while one was open for 4% -> 0% of each run, Pallas kernels for 0% -> 0%
where the time goes in v1:
time: 219 us; the launch traced here: 218 us
  Pallas kernels  211 us (96%)
  local copies, waits for them, and re-layouts  7.08 us (3%)
    pallas_call x1, Pallas kernels, shards(): pl.pallas_call(kernel, out_shape=[jax.ShapeDtypeStruct((512, 512), BF), j...  211 us
    unnamed x8, local copies, waits for them, and re-layouts  7.08 us

profile of v1, /device:TPU:6, one launch (start us, length us, event | category | flops | bytes accessed | tf_op | source)
XLA Modules:
  0.0 218.4 jit_solution(5641890738615548841)
XLA Ops:
  0.6 210.6 %shard_map.84 = (bf16[512,512]{1,0:T(8,128)(2,1)}, f32[1024,512]{1,0:T(8,128)}, f32[1024,512]{1,0:T(8,128)}, f32[64,512]{1,0:T(8,128)}) custom-call(bf16[64,512]{1,0:T(8,128)(2,1)} %bitcast.17, bf16[512,512]{1,0:T(8,128)(2,1)} %bitcast.15, bf16[512,512]{1,0:T(8,128)(2,1)} %bitcast.16, bf16[1024,512]{1,0:T(8,128)(2,1)} %bitcast.13, bf16[1024,512]{1,0:T(8,128)(2,1)} %bitcast.14), custom_call_target="tpu_custom_call" | custom-call | flops 14200000512 | bytes 8000000 | tf_op jit(solution)/shard_map/pallas_call | solution.py:426
  211.3 1.9 copy.13
  213.1 0.0 copy-start
  213.1 3.2 %copy.14 = f32[1,1024,512]{2,1,0:T(8,128)} copy(f32[1,1024,512]{2,1,0:T(8,128)} %bitcast.10) | data formatting | bytes 4194304
  216.4 0.0 copy-done
  216.4 0.0 copy-start.1
  216.4 1.3 copy.15
  217.7 0.0 copy-done.1
  217.7 0.7 copy.16
Async XLA Ops:
  213.1 3.2 %copy-start = (f32[1024,512]{1,0:T(8,128)S(1)}, f32[1024,512]{1,0:T(8,128)}, u32[]{:S(2)}) copy-start(f32[1024,512]{1,0:T(8,128)} %get-tuple-element.10) | copy-start | bytes 6291460
  216.4 1.3 copy-start.1

commit v2 on v0

v2 whole, which is shorter than its diff:
```python
import math

import jax
import jax.numpy as jnp
from jax import lax
from jax.experimental import pallas as pl
from jax.experimental.pallas import tpu as pltpu
from jax.sharding import PartitionSpec as P

DH = 256
BF = jnp.bfloat16
F32 = jnp.float32
MESH = pl.DeviceIdType.MESH
NT = (((1,), (1,)), ((), ()))
TN = (((0,), (0,)), ((), ()))


def mm(a, b):
    return jnp.dot(a, b, preferred_element_type=F32)


def kernel(
    enc, q, ctx, wk, wv,
    qg, gk, gv, eg,
    encg, enc2, enct, wbuf, psk, psv, prk, prv, pown, krow, vrow, att, sl, al, kvg, kvg2,
    dacc, dsend, drecv, r1, ra_a, ra_b, r2a, r2b, rb_a, rb_b, fin, frecv,
    ssem, rsem, lsem,
):
    pi = lax.axis_index("pipe")
    ti = lax.axis_index("tensor")
    d = lax.axis_index("dp")
    y, c = pi // 2, pi % 2
    x, zh = ti // 2, ti % 2
    xh, xl = x // 2, x % 2
    dh, dl = d // 2, d % 2
    oc, oh, ol = 1 - c, 1 - dh, 1 - dl
    scale = 1.0 / math.sqrt(DH)
    mine = xl * 2 + xh
    lo, hi = pl.ds(0, 32), pl.ds(32, 32)

    def at(xx, zz, dd):
        return (pi, xx * 2 + zz, dd)

    def xpeer(k):
        return at((x + k) % 4, zh, d)

    def ypeer(k):
        return (((y + k) % 4) * 2 + c, ti, d)

    def xblock(k):
        xx = (x + k) % 4
        return (xx % 2) * 2 + xx // 2

    peer_c = (y * 2 + oc, ti, d)
    peer_l = at(x, zh, dh * 2 + ol)
    peer_h = at(x, zh, oh * 2 + dl)
    to_plane = [at(zh * 2 + xl, z, xh * 2 + dl) for z in range(2)]
    from_own = at(dh * 2 + xl, xh, dh * 2 + dl)
    from_oth = at(dh * 2 + xl, xh, oh * 2 + dl)
    loop = jnp.logical_and(xh == dh, zh == xh)
    more = dl != xl
    to_more = [at(dh * 2 + zh, z, xh * 2 + xl) for z in range(2)]
    from_more = at(dh * 2 + dl, xl, xh * 2 + ol)

    used = [0]

    def take(n=1):
        used[0] += n
        return used[0] - n

    def send(src, dst, dev, k=None):
        k = take() if k is None else k
        return pltpu.make_async_remote_copy(
            src, dst, ssem.at[k], rsem.at[k], device_id=dev, device_id_type=MESH
        )

    def two_sems(src, dst, dev, ks, kr):
        return pltpu.make_async_remote_copy(
            src, dst, ssem.at[ks], rsem.at[kr], device_id=dev, device_id_type=MESH
        )

    barrier = pltpu.get_barrier_semaphore()

    def greet(dev):
        pl.semaphore_signal(barrier, inc=1, device_id=dev, device_id_type=MESH)

    peers = [peer_c, peer_l, peer_h]
    peers += [xpeer(k) for k in (1, 2, 3)] + [ypeer(k) for k in (1, 2, 3)]
    for dev in peers:
        greet(dev)
    greet(from_oth)
    greet(from_more)

    @pl.when(jnp.logical_not(loop))
    def _():
        greet(from_own)

    for z in range(2):

        @pl.when(jnp.logical_not(jnp.logical_and(loop, zh == z)))
        def _(z=z):
            greet(to_plane[z])

    owns = []
    for h in range(2):
        for kv, w in enumerate((wk, wv)):
            cp = pltpu.make_async_copy(
                w.at[:, pl.ds(h * DH, DH)], wbuf.at[h, kv, dl], lsem.at[h * 2 + kv]
            )
            cp.start()
            owns.append(cp)

    pl.semaphore_wait(
        barrier, len(peers) + jnp.where(loop, 2, 4) + jnp.where(more, 2, 0)
    )

    ks, kr = take(2), take(2)
    piece = encg.at[dh, xl * 2 + zh, y, c]
    out_piece = [two_sems(enc, piece, to_plane[z], ks + z, kr + dh) for z in range(2)]
    for z in range(2):

        @pl.when(jnp.logical_not(jnp.logical_and(loop, zh == z)))
        def _(z=z):
            out_piece[z].start()

    @pl.when(loop)
    def _():
        encg[dh, mine, y, c] = enc[...]

    ks2, kr2 = take(2), take(1)
    extra = enc2.at[dh, zh, y, c]
    out_more = [two_sems(enc, extra, to_more[z], ks2 + z, kr2) for z in range(2)]

    @pl.when(more)
    def _():
        for z in range(2):
            out_more[z].start()

    wsend = [
        [send(w.at[:, pl.ds(h * DH, DH)], wbuf.at[h, kv, dl], peer_l) for kv, w in enumerate((wk, wv))]
        for h in range(2)
    ]
    wsend[0][0].start()

    def piece_in(s):
        return two_sems(enc, encg.at[s, mine, y, c], from_oth, ks, kr + s)

    def gather_one(s):
        cps = []
        for k in (1, 2, 3):
            ref = encg.at[s, mine, y, c, lo]
            cps.append(send(ref, ref, xpeer(k)))
            ref = encg.at[s, mine, y, c, hi]
            cps.append(send(ref, ref, ypeer(k)))
        for cp in cps:
            cp.start()
        return cps

    def gather_two(s):
        cps = []
        for k in (1, 2, 3):
            ref = encg.at[s, :, y, c, lo]
            cps.append(send(ref, ref, ypeer(k)))
            ref = encg.at[s, mine, :, c, hi]
            cps.append(send(ref, ref, xpeer(k)))
        for cp in cps:
            cp.start()
        return cps

    def gather_core(s):
        ref = encg.at[s, :, :, c]
        cp = send(ref, ref, peer_c)
        cp.start()
        return cp

    def wait_all(cps):
        for cp in cps:
            cp.wait()

    piece_in(oh).wait_recv()
    g1o = gather_one(oh)

    @pl.when(jnp.logical_not(loop))
    def _():
        piece_in(dh).wait_recv()

    g1d = gather_one(dh)
    for z in range(2):

        @pl.when(jnp.logical_not(jnp.logical_and(loop, zh == z)))
        def _(z=z):
            out_piece[z].wait_send()

    wait_all(g1o)
    g2o = gather_two(oh)
    wsend[0][1].start()
    wait_all(g1d)
    wait_all(g2o)
    g3o = gather_core(oh)
    g2d = gather_two(dh)
    g3o.wait()

    def enc_rows(s, r):
        blocks = [encg[s, fb, pl.ds(r * 2, 2)].reshape(256, 512) for fb in range(4)]
        return jnp.concatenate(blocks, axis=1)

    def project(s, h, kv, put):
        def step(r, carry):
            w = wbuf[h, kv].reshape(2048, DH)
            put(pl.ds(pl.multiple_of(r * 256, 256), 256), mm(enc_rows(s, r), w))
            return carry

        lax.fori_loop(0, 2, step, 0)

    part = []

    def project_send(h, kv):
        owns[h * 2 + kv].wait()
        wsend[h][kv].wait()

        def put_k(rows, v):
            psk[h, rows, :] = v

        def put_v(rows, v):
            psv[h, rows, :] = v.astype(BF)

        project(oh, h, kv, put_v if kv else put_k)
        cp = send(psv.at[h], prv.at[h], peer_h) if kv else send(psk.at[h], prk.at[h], peer_h)
        cp.start()
        part.append(cp)

    def project_own(h, kv):
        def put(rows, v):
            pown[h, kv, rows, :] = v

        project(dh, h, kv, put)

    project_send(0, 0)
    wsend[1][0].start()
    project_send(0, 1)
    wsend[1][1].start()
    wait_all(g2d)
    g3d = gather_core(dh)

    @pl.when(more)
    def _():
        for z in range(2):
            out_more[z].wait_send()

    two_sems(enc, enc2.at[xh, xl, y, c], from_more, ks2, kr2).wait_recv()
    m1 = []
    for k in (1, 2, 3):
        ref = enc2.at[xh, xl, y, c]
        m1.append(send(ref, ref, xpeer(k)))
    for cp in m1:
        cp.start()
    g3d.wait()
    project_own(0, 0)
    project_own(0, 1)

    def flip(n, carry):
        s, z = n // 2, n % 2
        enct[s, z] = encg[s, dl * 2 + z].reshape(512, 512).T
        return carry

    lax.fori_loop(0, 4, flip, 0)
    project_send(1, 0)
    project_own(1, 0)
    project_send(1, 1)
    project_own(1, 1)
    wait_all(m1)
    m2 = []
    for k in (1, 2, 3):
        ref = enc2.at[:, :, y, c]
        m2.append(send(ref, ref, ypeer(k)))
    for cp in m2:
        cp.start()

    def flip2(n, carry):
        s, z = n // 2, n % 2
        enct[2 + s, z] = enc2[s, z].reshape(512, 512).T
        return carry

    grads = {}
    near = {}

    def grad_send(h, kv):
        ref = kvg.at[h, dh, kv]
        grads[h, kv] = send(ref, ref, peer_h)
        grads[h, kv].start()
        near[h, kv] = send(ref, kvg2.at[h, dh, kv], peer_l)
        near[h, kv].start()

    def attend(h):
        cols = pl.ds(h * DH, DH)
        part[2 * h].wait()
        krow[h] = (pown[h, 0] + prk[h]).astype(BF)

        def soft(r, carry):
            rows = pl.ds(pl.multiple_of(r * 128, 128), 128)
            s = lax.dot_general(q[rows, cols], krow[h], NT, preferred_element_type=F32) * scale
            e = jnp.exp(s - jnp.max(s, axis=-1, keepdims=True))
            a = e / jnp.sum(e, axis=-1, keepdims=True)
            att[rows, :] = a
            al[rows, :] = a.astype(BF)
            return carry

        lax.fori_loop(0, 4, soft, 0)
        kvg[h, dh, 1] = lax.dot_general(
            al[...], ctx[:, cols], TN, preferred_element_type=F32
        ).astype(BF)
        grad_send(h, 1)
        part[2 * h + 1].wait()
        vrow[h] = (pown[h, 1] + prv[h].astype(F32)).astype(BF)

        def back(r, carry):
            rows = pl.ds(pl.multiple_of(r * 128, 128), 128)
            a = att[rows, :]
            p = lax.dot_general(ctx[rows, cols], vrow[h], NT, preferred_element_type=F32)
            g = a * (p - jnp.sum(p * a, axis=-1, keepdims=True))
            low = (g * scale).astype(BF)
            sl[rows, :] = low
            qg[rows, cols] = mm(low, krow[h]).astype(BF)
            return carry

        lax.fori_loop(0, 4, back, 0)
        kvg[h, dh, 0] = lax.dot_general(
            sl[...], q[:, cols], TN, preferred_element_type=F32
        ).astype(BF)
        grad_send(h, 0)

    attend(0)
    wait_all(m2)
    ref = enc2.at[:, :, :, c]
    m3 = send(ref, ref, peer_c)
    m3.start()
    attend(1)

    far = {}

    def forward(h, kv):
        grads[h, kv].wait()
        far[h, kv] = send(kvg.at[h, oh, kv], kvg2.at[h, oh, kv], peer_l)
        far[h, kv].start()

    def weight_rows(fb, terms):
        qt, half = fb // 2, pl.ds(pl.multiple_of((fb % 2) * 512, 512), 512)
        return jnp.concatenate([wbuf[h, kv, qt, half, :] for h, kv in terms], axis=1)

    def encoder_term(s, terms, add, out):
        def step(fb, carry):
            both = jnp.concatenate([kvg[h, s, kv] for h, kv in terms], axis=1)
            v = lax.dot_general(both, weight_rows(fb, terms), NT, preferred_element_type=F32)
            v = v.reshape(4, 2, 64, 512)
            dacc[s, fb] = dacc[s, fb] + v if add else v
            if out:
                dsend[s, fb] = dacc[s, fb, :, oc].astype(BF)
            return carry

        lax.fori_loop(0, 4, step, 0)

    def reduce_core(s):
        cp = send(dsend.at[s], drecv.at[s], peer_c)
        cp.start()
        return cp

    def reduce_one(s, cp):
        cp.wait()

        def fold(n, carry):
            fb, yy = n // 4, n % 4
            r1[s, fb, yy] = (dacc[s, fb, yy, c] + drecv[s, fb, yy].astype(F32)).astype(BF)
            return carry

        lax.fori_loop(0, 16, fold, 0)
        cps = []
        for k in (1, 2, 3):
            cps.append(send(r1.at[s, xblock(k), :, lo], ra_a.at[s, k - 1], xpeer(k)))
            cps.append(send(r1.at[s, :, (y + k) % 4, hi], ra_b.at[s, k - 1], ypeer(k)))
        for cp in cps:
            cp.start()
        return cps

    def reduce_two(s, cps):
        wait_all(cps)

        def fold(n, carry):
            v = r1[s, mine, n, 0:32, :].astype(F32)
            w = r1[s, n, y, 32:64, :].astype(F32)
            for k in range(3):
                v = v + ra_a[s, k, n].astype(F32)
                w = w + ra_b[s, k, n].astype(F32)
            r2a[s, n] = v.astype(BF)
            r2b[s, n] = w.astype(BF)
            return carry

        lax.fori_loop(0, 4, fold, 0)
        cps = []
        for k in (1, 2, 3):
            cps.append(send(r2a.at[s, (y + k) % 4], rb_a.at[s, k - 1], ypeer(k)))
            cps.append(send(r2b.at[s, xblock(k)], rb_b.at[s, k - 1], xpeer(k)))
        for cp in cps:
            cp.start()
        return cps

    def reduce_sum(s, cps):
        wait_all(cps)
        v = r2a[s, y].astype(F32)
        w = r2b[s, mine].astype(F32)
        for k in range(3):
            v = v + rb_a[s, k].astype(F32)
            w = w + rb_b[s, k].astype(F32)
        fin[s, 0:32, :] = v
        fin[s, 32:64, :] = w

    def weight_term(h, first):
        cols = pl.ds(h * DH, DH)

        def step(z, carry):
            rows = pl.ds(pl.multiple_of(z * 512, 512), 512)
            base, buf = (0, kvg) if first else (2, kvg2)
            lhs = jnp.concatenate([enct[base, z], enct[base + 1, z]], axis=1)
            rhs = jnp.concatenate(
                [jnp.concatenate([buf[h, s, 0], buf[h, s, 1]], axis=1) for s in range(2)], axis=0
            )
            v = mm(lhs, rhs)
            if first:
                gk[rows, cols] = v[:, :DH]
                gv[rows, cols] = v[:, DH:]
            else:
                gk[rows, cols] += v[:, :DH]
                gv[rows, cols] += v[:, DH:]
            return carry

        lax.fori_loop(0, 2, step, 0)

    every = [(0, 0), (0, 1), (1, 1), (1, 0)]
    encoder_term(dh, every, False, True)
    rc = reduce_core(dh)
    rs = reduce_one(dh, rc)
    m3.wait()
    lax.fori_loop(0, 4, flip2, 0)
    forward(0, 1)
    forward(0, 0)
    rs = reduce_two(dh, rs)
    weight_term(0, True)
    reduce_sum(dh, rs)
    kf, krf = take(2), take(2)
    slot = frecv.at[zh]
    out_own = two_sems(fin.at[dh], slot, from_own, kf, krf + zh)
    out_oth = two_sems(fin.at[oh], slot, from_oth, kf + 1, krf + zh)

    @pl.when(jnp.logical_not(loop))
    def _():
        out_own.start()

    @pl.when(loop)
    def _():
        frecv[zh] = fin[dh]

    forward(1, 1)
    encoder_term(oh, every[:3], False, False)
    forward(1, 0)
    encoder_term(oh, every[3:], True, True)
    rc = reduce_core(oh)
    weight_term(1, True)
    rs = reduce_one(oh, rc)
    for kv in (1, 0):
        near[0, kv].wait()
        far[0, kv].wait()
    weight_term(0, False)
    rs = reduce_two(oh, rs)
    reduce_sum(oh, rs)
    out_oth.start()
    for kv in (1, 0):
        near[1, kv].wait()
        far[1, kv].wait()
    weight_term(1, False)

    @pl.when(jnp.logical_not(loop))
    def _():
        out_own.wait_send()

    out_oth.wait_send()
    for z in range(2):

        @pl.when(jnp.logical_not(jnp.logical_and(loop, zh == z)))
        def _(z=z):
            two_sems(fin.at[0], frecv.at[z], to_plane[z], kf, krf + z).wait_recv()

    eg[...] = frecv[0] + frecv[1]


def shards(encoder_out, queries, ctx_grad, key_weight, value_weight):
    vm = pl.BlockSpec(memory_space=pltpu.VMEM)
    hbm = pl.BlockSpec(memory_space=pl.ANY)
    scratch = [
        ((2, 4, 4, 2, 64, 512), BF),
        ((2, 2, 4, 2, 64, 512), BF),
        ((4, 2, 512, 512), BF),
        ((2, 2, 2, 1024, DH), BF),
        ((2, 512, DH), F32),
        ((2, 512, DH), BF),
        ((2, 512, DH), F32),
        ((2, 512, DH), BF),
        ((2, 2, 512, DH), F32),
        ((2, 512, DH), BF),
        ((2, 512, DH), BF),
        ((512, 512), F32),
        ((512, 512), BF),
        ((512, 512), BF),
        ((2, 2, 2, 512, DH), BF),
        ((2, 2, 2, 512, DH), BF),
        ((2, 4, 4, 2, 64, 512), F32),
        ((2, 4, 4, 64, 512), BF),
        ((2, 4, 4, 64, 512), BF),
        ((2, 4, 4, 64, 512), BF),
        ((2, 3, 4, 32, 512), BF),
        ((2, 3, 4, 32, 512), BF),
        ((2, 4, 32, 512), BF),
        ((2, 4, 32, 512), BF),
        ((2, 3, 32, 512), BF),
        ((2, 3, 32, 512), BF),
        ((2, 64, 512), F32),
        ((2, 64, 512), F32),
    ]
    qg, gk, gv, eg = pl.pallas_call(
        kernel,
        out_shape=[
            jax.ShapeDtypeStruct((512, 512), BF),
            jax.ShapeDtypeStruct((1024, 512), F32),
            jax.ShapeDtypeStruct((1024, 512), F32),
            jax.ShapeDtypeStruct((64, 512), F32),
        ],
        in_specs=[vm, vm, vm, hbm, hbm],
        out_specs=[vm, vm, vm, vm],
        scratch_shapes=[pltpu.VMEM(*s) for s in scratch]
        + [
            pltpu.SemaphoreType.DMA((96,)),
            pltpu.SemaphoreType.DMA((96,)),
            pltpu.SemaphoreType.DMA((4,)),
        ],
        compiler_params=pltpu.CompilerParams(
            collective_id=0, has_side_effects=True, vmem_limit_bytes=60 * 1024 * 1024
        ),
        cost_estimate=pl.CostEstimate(
            flops=14_200_000_000, bytes_accessed=8_000_000, transcendentals=600_000
        ),
    )(encoder_out[0], queries[0, 0], ctx_grad[0, 0], key_weight[0], value_weight[0])
    return qg[None, None], gk[None], gv[None], eg[None]


def solution(mesh):
    in_specs = (
        P("dp", "pipe", "tensor"),
        P("pipe", "dp", None, "tensor"),
        P("pipe", "dp", None, "tensor"),
        P("pipe", "dp", "tensor"),
        P("pipe", "dp", "tensor"),
    )
    out_specs = (
        P("pipe", "dp", None, "tensor"),
        P("pipe", "dp", "tensor"),
        P("pipe", "dp", "tensor"),
        P("dp", "pipe", "tensor"),
    )
    return jax.shard_map(shards, mesh=mesh, in_specs=in_specs, out_specs=out_specs, check_vma=False)
```

time: 906 us -> 187 us (0.21); the launches traced: 893 us -> 187 us
  waiting for transfers between devices: 754 us -> 0 us
  Pallas kernels: 0 us -> 179 us
  blocking collectives: 54 us -> 0 us
  matrix products: 47.2 us -> 0 us
  between operations: 13.9 us -> 0.64 us
  other arithmetic: 10 us -> 0 us
    reduce_scatter x2 -> x0, waiting for transfers between devices: 591 us -> none  [the longest x1 461 us: shards(): lax.psum_scatter(flat_term, ('pipe', 'tensor'), scatter_dimension=0, tile...]
    pallas_call x0 -> x1, Pallas kernels: none -> 179 us  [shards(): pl.pallas_call(kernel, out_shape=[jax.ShapeDtypeStruct((512, 512), BF), j...]
    all_gather x3 -> x0, waiting for transfers between devices: 161 us -> none  [the longest x1 79.4 us: shards(): lax.all_gather(key_weight[0], 'dp', axis=0, tiled=True)]
    all_gather x1 -> x0, blocking collectives: 54 us -> none  [shards(): widened = lax.all_gather(encoder_out, 'tensor', axis=2, tiled=True)]
    dot_general x10 -> x0, matrix products: 43.9 us -> none  [the longest x1 6.86 us: shards(): lax.dot_general(enc_flat, value_flat, contract, preferred_element_type=jn...]
  transfers between devices with their start and end apart: 5 -> 0, of which waited for: 5 -> 0; matrix products, arithmetic and copies ran while one was open for 4% -> 0% of each run, Pallas kernels for 0% -> 0%
where the time goes in v2:
time: 187 us
  Pallas kernels  179 us (96%)
  local copies, waits for them, and re-layouts  7.08 us (4%)
    pallas_call x1, Pallas kernels, shards(): pl.pallas_call(kernel, out_shape=[jax.ShapeDtypeStruct((512, 512), BF), j...  179 us
    unnamed x8, local copies, waits for them, and re-layouts  7.08 us

profile of v2, /device:TPU:6, one launch (start us, length us, event | category | flops | bytes accessed | tf_op | source)
XLA Modules:
  0.0 186.8 jit_solution(486053111291505881)
XLA Ops:
  0.6 179.1 %shard_map.84 = (bf16[512,512]{1,0:T(8,128)(2,1)}, f32[1024,512]{1,0:T(8,128)}, f32[1024,512]{1,0:T(8,128)}, f32[64,512]{1,0:T(8,128)}) custom-call(bf16[64,512]{1,0:T(8,128)(2,1)} %bitcast.17, bf16[512,512]{1,0:T(8,128)(2,1)} %bitcast.15, bf16[512,512]{1,0:T(8,128)(2,1)} %bitcast.16, bf16[1024,512]{1,0:T(8,128)(2,1)} %bitcast.13, bf16[1024,512]{1,0:T(8,128)(2,1)} %bitcast.14), custom_call_target="tpu_custom_call" | custom-call | flops 14200000512 | bytes 8000000 | tf_op jit(solution)/shard_map/pallas_call | solution.py:527
  179.8 1.9 %copy.13 = bf16[1,1,512,512]{3,2,1,0:T(8,128)(2,1)} copy(bf16[1,1,512,512]{3,2,1,0:T(8,128)(2,1)} %bitcast.11) | data formatting | bytes 1048576
  181.6 0.0 copy-start
  181.6 3.2 %copy.14 = f32[1,1024,512]{2,1,0:T(8,128)} copy(f32[1,1024,512]{2,1,0:T(8,128)} %bitcast.10) | data formatting | bytes 4194304
  184.9 0.0 copy-done
  184.9 0.0 copy-start.1
  184.9 1.3 copy.15
  186.2 0.0 copy-done.1
  186.2 0.7 copy.16
Async XLA Ops:
  181.6 3.2 %copy-start = (f32[1024,512]{1,0:T(8,128)S(1)}, f32[1024,512]{1,0:T(8,128)}, u32[]{:S(2)}) copy-start(f32[1024,512]{1,0:T(8,128)} %get-tuple-element.10) | copy-start | bytes 6291460
  184.9 1.3 copy-start.1

commit v3 on v2

--- a/solution.py
+++ b/solution.py
@@ -21,8 +21,8 @@
 
 def kernel(
     enc, q, ctx, wk, wv,
-    qg, gk, gv, eg,
-    encg, enc2, enct, wbuf, psk, psv, prk, prv, pown, krow, vrow, att, sl, al, kvg, kvg2,
+    qg_out, gk_out, gv_out, eg,
+    qg, gkv, encg, enc2, enct, wbuf, psk, psv, prk, prv, pown, krow, vrow, att, sl, al, kvg, kvg2,
     dacc, dsend, drecv, r1, ra_a, ra_b, r2a, r2b, rb_a, rb_b, fin, frecv,
     ssem, rsem, lsem,
 ):
@@ -131,11 +131,6 @@
     extra = enc2.at[dh, zh, y, c]
     out_more = [two_sems(enc, extra, to_more[z], ks2 + z, kr2) for z in range(2)]
 
-    @pl.when(more)
-    def _():
-        for z in range(2):
-            out_more[z].start()
-
     wsend = [
         [send(w.at[:, pl.ds(h * DH, DH)], wbuf.at[h, kv, dl], peer_l) for kv, w in enumerate((wk, wv))]
         for h in range(2)
@@ -184,6 +179,11 @@
     def _():
         piece_in(dh).wait_recv()
 
+    @pl.when(more)
+    def _():
+        for z in range(2):
+            out_more[z].start()
+
     g1d = gather_one(dh)
     for z in range(2):
 
@@ -198,44 +198,49 @@
     wait_all(g2o)
     g3o = gather_core(oh)
     g2d = gather_two(dh)
-    g3o.wait()
-
-    def enc_rows(s, r):
-        blocks = [encg[s, fb, pl.ds(r * 2, 2)].reshape(256, 512) for fb in range(4)]
-        return jnp.concatenate(blocks, axis=1)
-
-    def project(s, h, kv, put):
-        def step(r, carry):
-            w = wbuf[h, kv].reshape(2048, DH)
-            put(pl.ds(pl.multiple_of(r * 256, 256), 256), mm(enc_rows(s, r), w))
-            return carry
-
-        lax.fori_loop(0, 2, step, 0)
-
-    part = []
+
+    def project_rows(s, h, kv, cc):
+        blocks = [encg[s, fb, :, cc].reshape(256, 512) for fb in range(4)]
+        v = mm(jnp.concatenate(blocks, axis=1), wbuf[h, kv].reshape(2048, DH))
+        return v.reshape(4, 64, DH)
+
+    part = {}
 
     def project_send(h, kv):
         owns[h * 2 + kv].wait()
         wsend[h][kv].wait()
 
-        def put_k(rows, v):
-            psk[h, rows, :] = v
-
-        def put_v(rows, v):
-            psv[h, rows, :] = v.astype(BF)
-
-        project(oh, h, kv, put_v if kv else put_k)
+        def step(cc, carry):
+            v = project_rows(oh, h, kv, cc)
+            if kv:
+                psv[h, :, cc] = v.astype(BF)
+            else:
+                psk[h, :, cc] = v
+            return carry
+
+        lax.fori_loop(0, 2, step, 0)
         cp = send(psv.at[h], prv.at[h], peer_h) if kv else send(psk.at[h], prk.at[h], peer_h)
         cp.start()
-        part.append(cp)
+        part[h, kv] = [cp]
 
     def project_own(h, kv):
-        def put(rows, v):
-            pown[h, kv, rows, :] = v
-
-        project(dh, h, kv, put)
-
-    project_send(0, 0)
+        def step(cc, carry):
+            pown[h, kv, :, cc] = project_rows(dh, h, kv, cc)
+            return carry
+
+        lax.fori_loop(0, 2, step, 0)
+
+    owns[0].wait()
+    wsend[0][0].wait()
+    halves = []
+    for cc in (c, oc):
+        if len(halves) == 1:
+            g3o.wait()
+        psk[0, :, cc] = project_rows(oh, 0, 0, cc)
+        ref = (psk.at[0, :, cc], prk.at[0, :, cc])
+        halves.append(send(*ref, peer_h))
+        halves[-1].start()
+    part[0, 0] = halves
     wsend[1][0].start()
     project_send(0, 1)
     wsend[1][1].start()
@@ -293,8 +298,8 @@
 
     def attend(h):
         cols = pl.ds(h * DH, DH)
-        part[2 * h].wait()
-        krow[h] = (pown[h, 0] + prk[h]).astype(BF)
+        wait_all(part[h, 0])
+        krow[h] = (pown[h, 0] + prk[h]).reshape(512, DH).astype(BF)
 
         def soft(r, carry):
             rows = pl.ds(pl.multiple_of(r * 128, 128), 128)
@@ -310,8 +315,8 @@
             al[...], ctx[:, cols], TN, preferred_element_type=F32
         ).astype(BF)
         grad_send(h, 1)
-        part[2 * h + 1].wait()
-        vrow[h] = (pown[h, 1] + prv[h].astype(F32)).astype(BF)
+        wait_all(part[h, 1])
+        vrow[h] = (pown[h, 1] + prv[h].astype(F32)).reshape(512, DH).astype(BF)
 
         def back(r, carry):
             rows = pl.ds(pl.multiple_of(r * 128, 128), 128)
@@ -354,64 +359,68 @@
             v = v.reshape(4, 2, 64, 512)
             dacc[s, fb] = dacc[s, fb] + v if add else v
             if out:
-                dsend[s, fb] = dacc[s, fb, :, oc].astype(BF)
+                for n in range(2):
+                    for half in range(2):
+                        rows = pl.ds(half * 32 + n * 16, 16)
+                        dsend[s, n, fb, :, half] = dacc[s, fb, :, oc, rows, :].astype(BF)
             return carry
 
         lax.fori_loop(0, 4, step, 0)
 
     def reduce_core(s):
-        cp = send(dsend.at[s], drecv.at[s], peer_c)
-        cp.start()
-        return cp
-
-    def reduce_one(s, cp):
-        cp.wait()
-
-        def fold(n, carry):
-            fb, yy = n // 4, n % 4
-            r1[s, fb, yy] = (dacc[s, fb, yy, c] + drecv[s, fb, yy].astype(F32)).astype(BF)
-            return carry
-
-        lax.fori_loop(0, 16, fold, 0)
-        cps = []
-        for k in (1, 2, 3):
-            cps.append(send(r1.at[s, xblock(k), :, lo], ra_a.at[s, k - 1], xpeer(k)))
-            cps.append(send(r1.at[s, :, (y + k) % 4, hi], ra_b.at[s, k - 1], ypeer(k)))
+        cps = [send(dsend.at[s, n], drecv.at[s, n], peer_c) for n in range(2)]
         for cp in cps:
             cp.start()
         return cps
 
-    def reduce_two(s, cps):
-        wait_all(cps)
-
-        def fold(n, carry):
-            v = r1[s, mine, n, 0:32, :].astype(F32)
-            w = r1[s, n, y, 32:64, :].astype(F32)
-            for k in range(3):
-                v = v + ra_a[s, k, n].astype(F32)
-                w = w + ra_b[s, k, n].astype(F32)
-            r2a[s, n] = v.astype(BF)
-            r2b[s, n] = w.astype(BF)
-            return carry
-
-        lax.fori_loop(0, 4, fold, 0)
+    def reduce_one(s, n, cp):
+        cp.wait()
+        for half in range(2):
+            rows = pl.ds(half * 32 + n * 16, 16)
+
+            def fold(fb, carry):
+                v = dacc[s, fb, :, c, rows, :] + drecv[s, n, fb, :, half].astype(F32)
+                r1[s, n, half, fb] = v.astype(BF)
+                return carry
+
+            lax.fori_loop(0, 4, fold, 0)
         cps = []
         for k in (1, 2, 3):
-            cps.append(send(r2a.at[s, (y + k) % 4], rb_a.at[s, k - 1], ypeer(k)))
-            cps.append(send(r2b.at[s, xblock(k)], rb_b.at[s, k - 1], xpeer(k)))
+            cps.append(send(r1.at[s, n, 0, xblock(k)], ra_a.at[s, n, k - 1], xpeer(k)))
+            cps.append(send(r1.at[s, n, 1, :, (y + k) % 4], ra_b.at[s, n, k - 1], ypeer(k)))
         for cp in cps:
             cp.start()
         return cps
 
-    def reduce_sum(s, cps):
+    def reduce_two(s, n, cps):
         wait_all(cps)
-        v = r2a[s, y].astype(F32)
-        w = r2b[s, mine].astype(F32)
+        v = r1[s, n, 0, mine].astype(F32)
+        w = r1[s, n, 1, :, y].astype(F32)
         for k in range(3):
-            v = v + rb_a[s, k].astype(F32)
-            w = w + rb_b[s, k].astype(F32)
-        fin[s, 0:32, :] = v
-        fin[s, 32:64, :] = w
+            v = v + ra_a[s, n, k].astype(F32)
+            w = w + ra_b[s, n, k].astype(F32)
+        r2a[s, n] = v.astype(BF)
+        r2b[s, n] = w.astype(BF)
+        cps = []
+        for k in (1, 2, 3):
+            cps.append(send(r2a.at[s, n, (y + k) % 4], rb_a.at[s, n, k - 1], ypeer(k)))
+            cps.append(send(r2b.at[s, n, xblock(k)], rb_b.at[s, n, k - 1], xpeer(k)))
+        for cp in cps:
+            cp.start()
+        return cps
+
+    def reduce_sum(s, n, cps):
+        wait_all(cps)
+        v = r2a[s, n, y].astype(F32)
+        w = r2b[s, n, mine].astype(F32)
+        for k in range(3):
+            v = v + rb_a[s, n, k].astype(F32)
+            w = w + rb_b[s, n, k].astype(F32)
+        fin[s, n, 0] = v.astype(BF)
+        fin[s, n, 1] = w.astype(BF)
+
+    done = [pltpu.make_async_copy(qg, qg_out, lsem.at[8])]
+    done[0].start()
 
     def weight_term(h, first):
         cols = pl.ds(h * DH, DH)
@@ -425,34 +434,40 @@
             )
             v = mm(lhs, rhs)
             if first:
-                gk[rows, cols] = v[:, :DH]
-                gv[rows, cols] = v[:, DH:]
+                gkv[h, 0, rows, :] = v[:, :DH]
+                gkv[h, 1, rows, :] = v[:, DH:]
             else:
-                gk[rows, cols] += v[:, :DH]
-                gv[rows, cols] += v[:, DH:]
+                gkv[h, 0, rows, :] += v[:, :DH]
+                gkv[h, 1, rows, :] += v[:, DH:]
             return carry
 
         lax.fori_loop(0, 2, step, 0)
+        if not first:
+            for kv, out in enumerate((gk_out, gv_out)):
+                done.append(pltpu.make_async_copy(gkv.at[h, kv], out.at[:, cols], lsem.at[4 + 2 * h + kv]))
+                done[-1].start()
 
     every = [(0, 0), (0, 1), (1, 1), (1, 0)]
     encoder_term(dh, every, False, True)
     rc = reduce_core(dh)
-    rs = reduce_one(dh, rc)
+    rs = [reduce_one(dh, n, rc[n]) for n in range(2)]
     m3.wait()
     lax.fori_loop(0, 4, flip2, 0)
     forward(0, 1)
     forward(0, 0)
-    rs = reduce_two(dh, rs)
+    rs = [reduce_two(dh, n, rs[n]) for n in range(2)]
     weight_term(0, True)
-    reduce_sum(dh, rs)
-    kf, krf = take(2), take(2)
-    slot = frecv.at[zh]
-    out_own = two_sems(fin.at[dh], slot, from_own, kf, krf + zh)
-    out_oth = two_sems(fin.at[oh], slot, from_oth, kf + 1, krf + zh)
+    for n in range(2):
+        reduce_sum(dh, n, rs[n])
+    kf, krf = take(4), take(4)
+
+    out_own = [two_sems(fin.at[dh, n], frecv.at[zh, n], from_own, kf + n, krf + 2 * n + zh) for n in range(2)]
+    out_oth = [two_sems(fin.at[oh, n], frecv.at[zh, n], from_oth, kf + 2 + n, krf + 2 * n + zh) for n in range(2)]
 
     @pl.when(jnp.logical_not(loop))
     def _():
-        out_own.start()
+        for cp in out_own:
+            cp.start()
 
     @pl.when(loop)
     def _():
@@ -463,15 +478,18 @@
     forward(1, 0)
     encoder_term(oh, every[3:], True, True)
     rc = reduce_core(oh)
+    rs = [reduce_one(oh, n, rc[n]) for n in range(2)]
     weight_term(1, True)
-    rs = reduce_one(oh, rc)
+    rs[0] = reduce_two(oh, 0, rs[0])
     for kv in (1, 0):
         near[0, kv].wait()
         far[0, kv].wait()
     weight_term(0, False)
-    rs = reduce_two(oh, rs)
-    reduce_sum(oh, rs)
-    out_oth.start()
+    rs[1] = reduce_two(oh, 1, rs[1])
+    reduce_sum(oh, 0, rs[0])
+    out_oth[0].start()
+    reduce_sum(oh, 1, rs[1])
+    out_oth[1].start()
     for kv in (1, 0):
         near[1, kv].wait()
         far[1, kv].wait()
@@ -479,31 +497,58 @@
 
     @pl.when(jnp.logical_not(loop))
     def _():
-        out_own.wait_send()
-
-    out_oth.wait_send()
+        for cp in out_own:
+            cp.wait_send()
+
+    for cp in out_oth:
+        cp.wait_send()
     for z in range(2):
 
         @pl.when(jnp.logical_not(jnp.logical_and(loop, zh == z)))
         def _(z=z):
-            two_sems(fin.at[0], frecv.at[z], to_plane[z], kf, krf + z).wait_recv()
-
-    eg[...] = frecv[0] + frecv[1]
+            for n in range(2):
+                two_sems(fin.at[0, n], frecv.at[z, n], to_plane[z], kf, krf + 2 * n + z).wait_recv()
+
+    for n in range(2):
+        for half in range(2):
+            v = frecv[0, n, half].astype(F32) + frecv[1, n, half].astype(F32)
+            eg[half * 32 + n * 16 : half * 32 + n * 16 + 16, :] = v
+    for cp in done:
+        cp.wait()
+
+
+def hand_over(*arrays):
+    n, steps = len(arrays), 2
+
+    def kernel(*refs):
+        for i in range(n):
+            refs[n + i][...] = refs[i][...]
+
+    specs = [pl.BlockSpec((a.shape[0] // steps, a.shape[1]), lambda i: (i, 0)) for a in arrays]
+    return pl.pallas_call(
+        kernel,
+        grid=(steps,),
+        out_shape=[jax.ShapeDtypeStruct(a.shape, a.dtype) for a in arrays],
+        in_specs=specs,
+        out_specs=specs,
+    )(*arrays)
 
 
 def shards(encoder_out, queries, ctx_grad, key_weight, value_weight):
     vm = pl.BlockSpec(memory_space=pltpu.VMEM)
     hbm = pl.BlockSpec(memory_space=pl.ANY)
     scratch = [
+        ((512, 512), BF),
+        ((2, 2, 1024, DH), F32),
         ((2, 4, 4, 2, 64, 512), BF),
         ((2, 2, 4, 2, 64, 512), BF),
         ((4, 2, 512, 512), BF),
         ((2, 2, 2, 1024, DH), BF),
-        ((2, 512, DH), F32),
-        ((2, 512, DH), BF),
-        ((2, 512, DH), F32),
-        ((2, 512, DH), BF),
-        ((2, 2, 512, DH), F32),
+        ((2, 4, 2, 64, DH), F32),
+        ((2, 4, 2, 64, DH), BF),
+        ((2, 4, 2, 64, DH), F32),
+        ((2, 4, 2, 64, DH), BF),
+        ((2, 2, 4, 2, 64, DH), F32),
         ((2, 512, DH), BF),
         ((2, 512, DH), BF),
         ((512, 512), F32),
@@ -512,17 +557,17 @@
         ((2, 2, 2, 512, DH), BF),
         ((2, 2, 2, 512, DH), BF),
         ((2, 4, 4, 2, 64, 512), F32),
-        ((2, 4, 4, 64, 512), BF),
-        ((2, 4, 4, 64, 512), BF),
-        ((2, 4, 4, 64, 512), BF),
-        ((2, 3, 4, 32, 512), BF),
-        ((2, 3, 4, 32, 512), BF),
-        ((2, 4, 32, 512), BF),
-        ((2, 4, 32, 512), BF),
-        ((2, 3, 32, 512), BF),
-        ((2, 3, 32, 512), BF),
-        ((2, 64, 512), F32),
-        ((2, 64, 512), F32),
+        ((2, 2, 4, 4, 2, 16, 512), BF),
+        ((2, 2, 4, 4, 2, 16, 512), BF),
+        ((2, 2, 2, 4, 4, 16, 512), BF),
+        ((2, 2, 3, 4, 16, 512), BF),
+        ((2, 2, 3, 4, 16, 512), BF),
+        ((2, 2, 4, 16, 512), BF),
+        ((2, 2, 4, 16, 512), BF),
+        ((2, 2, 3, 16, 512), BF),
+        ((2, 2, 3, 16, 512), BF),
+        ((2, 2, 2, 16, 512), BF),
+        ((2, 2, 2, 16, 512), BF),
     ]
     qg, gk, gv, eg = pl.pallas_call(
         kernel,
@@ -533,12 +578,12 @@
             jax.ShapeDtypeStruct((64, 512), F32),
         ],
         in_specs=[vm, vm, vm, hbm, hbm],
-        out_specs=[vm, vm, vm, vm],
+        out_specs=[hbm, hbm, hbm, vm],
         scratch_shapes=[pltpu.VMEM(*s) for s in scratch]
         + [
-            pltpu.SemaphoreType.DMA((96,)),
-            pltpu.SemaphoreType.DMA((96,)),
-            pltpu.SemaphoreType.DMA((4,)),
+            pltpu.SemaphoreType.DMA((160,)),
+            pltpu.SemaphoreType.DMA((160,)),
+            pltpu.SemaphoreType.DMA((9,)),
         ],
         compiler_params=pltpu.CompilerParams(
             collective_id=0, has_side_effects=True, vmem_limit_bytes=60 * 1024 * 1024
@@ -547,6 +592,7 @@
             flops=14_200_000_000, bytes_accessed=8_000_000, transcendentals=600_000
         ),
     )(encoder_out[0], queries[0, 0], ctx_grad[0, 0], key_weight[0], value_weight[0])
+    qg, gk, gv, eg = hand_over(qg, gk, gv, eg)
     return qg[None, None], gk[None], gv[None], eg[None]
 
 

time: 187 us -> 179 us (0.957)
  local copies, waits for them, and re-layouts: 7.08 us -> 0 us
    unnamed x8 -> x0, local copies, waits for them, and re-layouts: 7.08 us -> none
    pallas_call x1, Pallas kernels: 179 us -> 174 us  [shards(): pl.pallas_call(kernel, out_shape=[jax.ShapeDtypeStruct((512, 512), BF), j...]
    pallas_call x0 -> x1, Pallas kernels: none -> 4 us  [hand_over(): pl.pallas_call(kernel, grid=(steps,), out_shape=[jax.ShapeDtypeStruct(a.s...]
where the time goes in v3:
time: 179 us
  Pallas kernels  178 us (99%)
    pallas_call x1, Pallas kernels, shards(): pl.pallas_call(kernel, out_shape=[jax.ShapeDtypeStruct((512, 512), BF), j...  174 us
    pallas_call x1, Pallas kernels, hand_over(): pl.pallas_call(kernel, grid=(steps,), out_shape=[jax.ShapeDtypeStruct(a.s...  4 us

profile of v3, /device:TPU:6, one launch (start us, length us, event | category | flops | bytes accessed | tf_op | source)
XLA Modules:
  0.0 178.9 jit_solution(6564891813884214736)
XLA Ops:
  0.6 174.2 %shard_map.84 = (bf16[512,512]{1,0:T(8,128)(2,1)}, f32[1024,512]{1,0:T(8,128)}, f32[1024,512]{1,0:T(8,128)}, f32[64,512]{1,0:T(8,128)}) custom-call(bf16[64,512]{1,0:T(8,128)(2,1)} %bitcast.17, bf16[512,512]{1,0:T(8,128)(2,1)} %bitcast.13, bf16[512,512]{1,0:T(8,128)(2,1)} %bitcast.14, bf16[1024,512]{1,0:T(8,128)(2,1)} %bitcast.11, bf16[1024,512]{1,0:T(8,128)(2,1)} %bitcast.12), custom_call_target="tpu_custom_call" | custom-call | flops 14200000512 | bytes 8000000 | tf_op jit(solution)/shard_map/pallas_call | solution.py:572
  174.9 4.0 %shard_map.85 = (bf16[512,512]{1,0:T(8,128)(2,1)}, f32[1024,512]{1,0:T(8,128)}, f32[1024,512]{1,0:T(8,128)}, f32[64,512]{1,0:T(8,128)}) custom-call(bf16[512,512]{1,0:T(8,128)(2,1)} %get-tuple-element.12.refs_0_, f32[1024,512]{1,0:T(8,128)} %get-tuple-element.13.refs_1_, f32[1024,512]{1,0:T(8,128)} %get-tuple-element.14.refs_2_, ...), custom_call_target="tpu_custom_call" | custom-call | tf_op jit(solution)/shard_map/pallas_call | solution.py:528

commit v4 on v3

--- a/solution.py
+++ b/solution.py
@@ -62,17 +62,28 @@
     to_more = [at(dh * 2 + zh, z, xh * 2 + xl) for z in range(2)]
     from_more = at(dh * 2 + dl, xl, xh * 2 + ol)
 
-    used = [0]
-
-    def take(n=1):
-        used[0] += n
-        return used[0] - n
-
-    def send(src, dst, dev, k=None):
-        k = take() if k is None else k
-        return pltpu.make_async_remote_copy(
-            src, dst, ssem.at[k], rsem.at[k], device_id=dev, device_id_type=MESH
-        )
+    used = {"send": 0, "recv": 0}
+    free = []
+
+    def take(kind, n=1):
+        used[kind] += n
+        return used[kind] - n
+
+    class Move:
+        def __init__(self, src, dst, dev):
+            self.k = free.pop() if free else take("send")
+            self.copy = pltpu.make_async_remote_copy(
+                src, dst, ssem.at[self.k], rsem.at[take("recv")], device_id=dev, device_id_type=MESH
+            )
+
+        def start(self):
+            self.copy.start()
+
+        def wait(self):
+            self.copy.wait()
+            free.append(self.k)
+
+    send = Move
 
     def two_sems(src, dst, dev, ks, kr):
         return pltpu.make_async_remote_copy(
@@ -114,7 +125,7 @@
         barrier, len(peers) + jnp.where(loop, 2, 4) + jnp.where(more, 2, 0)
     )
 
-    ks, kr = take(2), take(2)
+    ks, kr = take("send", 2), take("recv", 2)
     piece = encg.at[dh, xl * 2 + zh, y, c]
     out_piece = [two_sems(enc, piece, to_plane[z], ks + z, kr + dh) for z in range(2)]
     for z in range(2):
@@ -127,7 +138,7 @@
     def _():
         encg[dh, mine, y, c] = enc[...]
 
-    ks2, kr2 = take(2), take(1)
+    ks2, kr2 = take("send", 2), take("recv")
     extra = enc2.at[dh, zh, y, c]
     out_more = [two_sems(enc, extra, to_more[z], ks2 + z, kr2) for z in range(2)]
 
@@ -457,27 +468,28 @@
     forward(0, 0)
     rs = [reduce_two(dh, n, rs[n]) for n in range(2)]
     weight_term(0, True)
-    for n in range(2):
-        reduce_sum(dh, n, rs[n])
-    kf, krf = take(4), take(4)
+    kf, krf = take("send", 4), take("recv", 4)
 
     out_own = [two_sems(fin.at[dh, n], frecv.at[zh, n], from_own, kf + n, krf + 2 * n + zh) for n in range(2)]
     out_oth = [two_sems(fin.at[oh, n], frecv.at[zh, n], from_oth, kf + 2 + n, krf + 2 * n + zh) for n in range(2)]
-
-    @pl.when(jnp.logical_not(loop))
-    def _():
-        for cp in out_own:
-            cp.start()
-
-    @pl.when(loop)
-    def _():
-        frecv[zh] = fin[dh]
 
     forward(1, 1)
     encoder_term(oh, every[:3], False, False)
     forward(1, 0)
     encoder_term(oh, every[3:], True, True)
     rc = reduce_core(oh)
+    for n in range(2):
+        reduce_sum(dh, n, rs[n])
+
+    @pl.when(jnp.logical_not(loop))
+    def _():
+        for cp in out_own:
+            cp.start()
+
+    @pl.when(loop)
+    def _():
+        frecv[zh] = fin[dh]
+
     rs = [reduce_one(oh, n, rc[n]) for n in range(2)]
     weight_term(1, True)
     rs[0] = reduce_two(oh, 0, rs[0])
@@ -581,8 +593,8 @@
         out_specs=[hbm, hbm, hbm, vm],
         scratch_shapes=[pltpu.VMEM(*s) for s in scratch]
         + [
-            pltpu.SemaphoreType.DMA((160,)),
-            pltpu.SemaphoreType.DMA((160,)),
+            pltpu.SemaphoreType.DMA((30,)),
+            pltpu.SemaphoreType.DMA((113,)),
             pltpu.SemaphoreType.DMA((9,)),
         ],
         compiler_params=pltpu.CompilerParams(

time: 179 us -> 177 us (0.989)
  Pallas kernels: 178 us -> 176 us
    pallas_call x1, Pallas kernels: 174 us -> 172 us  [shards(): pl.pallas_call(kernel, out_shape=[jax.ShapeDtypeStruct((512, 512), BF), j...]
where the time goes in v4:
time: 177 us
  Pallas kernels  176 us (99%)
    pallas_call x1, Pallas kernels, shards(): pl.pallas_call(kernel, out_shape=[jax.ShapeDtypeStruct((512, 512), BF), j...  172 us
    pallas_call x1, Pallas kernels, hand_over(): pl.pallas_call(kernel, grid=(steps,), out_shape=[jax.ShapeDtypeStruct(a.s...  4 us

profile of v4, /device:TPU:6, one launch (start us, length us, event | category | flops | bytes accessed | tf_op | source)
XLA Modules:
  0.0 176.8 jit_solution(6682021152051952052)
XLA Ops:
  0.6 172.1 %shard_map.84 = (bf16[512,512]{1,0:T(8,128)(2,1)}, f32[1024,512]{1,0:T(8,128)}, f32[1024,512]{1,0:T(8,128)}, f32[64,512]{1,0:T(8,128)}) custom-call(bf16[64,512]{1,0:T(8,128)(2,1)} %bitcast.17, bf16[512,512]{1,0:T(8,128)(2,1)} %bitcast.13, bf16[512,512]{1,0:T(8,128)(2,1)} %bitcast.14, bf16[1024,512]{1,0:T(8,128)(2,1)} %bitcast.11, bf16[1024,512]{1,0:T(8,128)(2,1)} %bitcast.12), custom_call_target="tpu_custom_call" | custom-call | flops 14200000512 | bytes 8000000 | tf_op jit(solution)/shard_map/pallas_call | solution.py:584
  172.8 4.0 %shard_map.85 = (bf16[512,512]{1,0:T(8,128)(2,1)}, f32[1024,512]{1,0:T(8,128)}, f32[1024,512]{1,0:T(8,128)}, f32[64,512]{1,0:T(8,128)}) custom-call(bf16[512,512]{1,0:T(8,128)(2,1)} %get-tuple-element.12.refs_0_, f32[1024,512]{1,0:T(8,128)} %get-tuple-element.13.refs_1_, f32[1024,512]{1,0:T(8,128)} %get-tuple-element.14.refs_2_, ...), custom_call_target="tpu_custom_call" | custom-call | tf_op jit(solution)/shard_map/pallas_call | solution.py:540

commit v5 on v4

--- a/solution.py
+++ b/solution.py
@@ -20,9 +20,9 @@
 
 
 def kernel(
-    enc, q, ctx, wk, wv,
+    enc, q_in, ctx_in, wk, wv,
     qg_out, gk_out, gv_out, eg,
-    qg, gkv, encg, enc2, enct, wbuf, psk, psv, prk, prv, pown, krow, vrow, att, sl, al, kvg, kvg2,
+    q, ctx, qg, gkv, encg, enc2, enct, wbuf, psk, psv, prk, prv, pown, krow, vrow, att, sl, al, kvg, kvg2,
     dacc, dsend, drecv, r1, ra_a, ra_b, r2a, r2b, rb_a, rb_b, fin, frecv,
     ssem, rsem, lsem,
 ):
@@ -134,9 +134,18 @@
         def _(z=z):
             out_piece[z].start()
 
+    stay = pltpu.make_async_copy(enc, encg.at[dh, mine, y, c], lsem.at[9])
+
     @pl.when(loop)
     def _():
-        encg[dh, mine, y, c] = enc[...]
+        stay.start()
+
+    inputs = [
+        pltpu.make_async_copy(q_in, q, lsem.at[10]),
+        pltpu.make_async_copy(ctx_in, ctx, lsem.at[11]),
+    ]
+    for cp in inputs:
+        cp.start()
 
     ks2, kr2 = take("send", 2), take("recv")
     extra = enc2.at[dh, zh, y, c]
@@ -194,6 +203,10 @@
     def _():
         for z in range(2):
             out_more[z].start()
+
+    @pl.when(loop)
+    def _():
+        stay.wait()
 
     g1d = gather_one(dh)
     for z in range(2):
@@ -345,6 +358,8 @@
         ).astype(BF)
         grad_send(h, 0)
 
+    for cp in inputs:
+        cp.wait()
     attend(0)
     wait_all(m2)
     ref = enc2.at[:, :, :, c]
@@ -466,14 +481,13 @@
     lax.fori_loop(0, 4, flip2, 0)
     forward(0, 1)
     forward(0, 0)
-    rs = [reduce_two(dh, n, rs[n]) for n in range(2)]
-    weight_term(0, True)
     kf, krf = take("send", 4), take("recv", 4)
 
     out_own = [two_sems(fin.at[dh, n], frecv.at[zh, n], from_own, kf + n, krf + 2 * n + zh) for n in range(2)]
     out_oth = [two_sems(fin.at[oh, n], frecv.at[zh, n], from_oth, kf + 2 + n, krf + 2 * n + zh) for n in range(2)]
 
     forward(1, 1)
+    rs = [reduce_two(dh, n, rs[n]) for n in range(2)]
     encoder_term(oh, every[:3], False, False)
     forward(1, 0)
     encoder_term(oh, every[3:], True, True)
@@ -491,6 +505,7 @@
         frecv[zh] = fin[dh]
 
     rs = [reduce_one(oh, n, rc[n]) for n in range(2)]
+    weight_term(0, True)
     weight_term(1, True)
     rs[0] = reduce_two(oh, 0, rs[0])
     for kv in (1, 0):
@@ -550,6 +565,8 @@
     vm = pl.BlockSpec(memory_space=pltpu.VMEM)
     hbm = pl.BlockSpec(memory_space=pl.ANY)
     scratch = [
+        ((512, 512), BF),
+        ((512, 512), BF),
         ((512, 512), BF),
         ((2, 2, 1024, DH), F32),
         ((2, 4, 4, 2, 64, 512), BF),
@@ -589,13 +606,13 @@
             jax.ShapeDtypeStruct((1024, 512), F32),
             jax.ShapeDtypeStruct((64, 512), F32),
         ],
-        in_specs=[vm, vm, vm, hbm, hbm],
+        in_specs=[hbm] * 5,
         out_specs=[hbm, hbm, hbm, vm],
         scratch_shapes=[pltpu.VMEM(*s) for s in scratch]
         + [
             pltpu.SemaphoreType.DMA((30,)),
             pltpu.SemaphoreType.DMA((113,)),
-            pltpu.SemaphoreType.DMA((9,)),
+            pltpu.SemaphoreType.DMA((12,)),
         ],
         compiler_params=pltpu.CompilerParams(
             collective_id=0, has_side_effects=True, vmem_limit_bytes=60 * 1024 * 1024

time: 177 us -> 176 us (level)
  no operation moved by 1% of the time
where the time goes in v5:
time: 176 us
  Pallas kernels  175 us (99%)
    pallas_call x1, Pallas kernels, shards(): pl.pallas_call(kernel, out_shape=[jax.ShapeDtypeStruct((512, 512), BF), j...  171 us
    pallas_call x1, Pallas kernels, hand_over(): pl.pallas_call(kernel, grid=(steps,), out_shape=[jax.ShapeDtypeStruct(a.s...  4 us

profile of v5, /device:TPU:6, one launch (start us, length us, event | category | flops | bytes accessed | tf_op | source)
XLA Modules:
  0.0 175.7 jit_solution(17991023893053776371)
XLA Ops:
  0.6 171.1 %shard_map.84 = (bf16[512,512]{1,0:T(8,128)(2,1)}, f32[1024,512]{1,0:T(8,128)}, f32[1024,512]{1,0:T(8,128)}, f32[64,512]{1,0:T(8,128)}) custom-call(bf16[64,512]{1,0:T(8,128)(2,1)} %bitcast.17, bf16[512,512]{1,0:T(8,128)(2,1)} %bitcast.13, bf16[512,512]{1,0:T(8,128)(2,1)} %bitcast.14, bf16[1024,512]{1,0:T(8,128)(2,1)} %bitcast.11, bf16[1024,512]{1,0:T(8,128)(2,1)} %bitcast.12), custom_call_target="tpu_custom_call" | custom-call | flops 14200000512 | bytes 8000000 | tf_op jit(solution)/shard_map/pallas_call | solution.py:601
  171.7 4.0 %shard_map.85 = (bf16[512,512]{1,0:T(8,128)(2,1)}, f32[1024,512]{1,0:T(8,128)}, f32[1024,512]{1,0:T(8,128)}, f32[64,512]{1,0:T(8,128)}) custom-call(bf16[512,512]{1,0:T(8,128)(2,1)} %get-tuple-element.12.refs_0_, f32[1024,512]{1,0:T(8,128)} %get-tuple-element.13.refs_1_, f32[1024,512]{1,0:T(8,128)} %get-tuple-element.14.refs_2_, ...), custom_call_target="tpu_custom_call" | custom-call | tf_op jit(solution)/shard_map/pallas_call | solution.py:555
